TPU v7x, 32 devices: a whole 2x2x4 slice. The times are simulated.
32 devices in a mesh: parts: 2 (over x), seq: 16 (over z, y, core).
Axes of the slice: x: 2, y: 2, z: 4, core: 2. Of those that a mesh axis runs over, the one named last changes fastest.
Arguments:
- control: bfloat16 [256, 3072], P(('parts', 'seq')), parts along dimension 0, may hold values from -6 to 6
- mask_ids: int32 [256], P(('parts', 'seq')), parts along dimension 0, may hold values from 0 to 2
- owner: int32 [256], P('parts'), parts along dimension 0, may hold values from 0 to 127, each once
- mask_table: bfloat16 [3, 3072], replicated, may hold values from -6 to 6
- res_weight: bfloat16 [3072, 3072], P(None, 'seq'), may hold values from -0.109375 to 0.109375
- base: bfloat16 [256, 3072], P(('parts', 'seq')), parts along dimension 0, may hold values from -6 to 6
- modulation: float32 [2, 3072], replicated, may hold values from -0.5 to 0.5
- q_weight: bfloat16 [3072, 1536], P(None, 'seq'), may hold values from -1 to 1
- k_weight: bfloat16 [3072, 1536], P(None, 'seq'), may hold values from -4 to 4
- v_weight: bfloat16 [3072, 1536], P(None, 'seq'), may hold values from -0.109375 to 0.109375
Outputs:
- hidden_out: bfloat16 [256, 3072], P(('parts', 'seq')), parts along dimension 0
- attended: bfloat16 [256, 1536], P(('parts', 'seq')), parts along dimension 0
There are 2 independent parts, one for each index of `parts`. A program takes and returns all parts, laid end to end along the dimension named above; an argument that names none is the same for every part. Nothing has to cross between parts.
Inputs may be any that keep to these rules, and one draw needn't show every extreme that they name: `owner`: each base row is named by exactly one control row.
All inputs are finite; a program needn't handle non-finite values.
Results may differ from a plain program's by a relative error of at most 0.006.
Values may be sent and summed in bfloat16 or wider, within the bound.
A program may use at most 64 MiB of HBM per device.

v0:
```python
import math

import jax
import jax.numpy as jnp
from jax import lax
from jax.sharding import PartitionSpec as P

HEADS = 12
HEAD_DIM = 128


def layer_norm(hidden, modulation):
    row_mean = jnp.mean(hidden, axis=1, keepdims=True)
    centred = hidden - row_mean
    row_var = jnp.mean(centred * centred, axis=1, keepdims=True)
    scaled = centred * lax.rsqrt(row_var + 1e-06)
    return (scaled * (1.0 + modulation[1]) + modulation[0]).astype(jnp.bfloat16)


def attend_block(carried, segments, query_heads):
    running_max, running_sum, summed = carried
    key_rows, values = segments
    block_rows = key_rows.shape[0]
    key_heads = key_rows.reshape(block_rows, HEADS, HEAD_DIM)
    value_heads = values.reshape(block_rows, HEADS, HEAD_DIM)
    scores = jnp.einsum(
        "thd,khd->thk", query_heads, key_heads, preferred_element_type=jnp.float32
    ) / math.sqrt(HEAD_DIM)
    new_max = jnp.maximum(running_max, jnp.max(scores, axis=2))
    weights = jnp.exp(scores - new_max[:, :, None])
    running_sum = jnp.sum(weights, axis=2)
    summed = jnp.einsum(
        "thk,khd->thd",
        weights.astype(jnp.bfloat16),
        value_heads,
        preferred_element_type=jnp.float32,
    )
    return (new_max, running_sum, summed)


def on_device(
    control, mask_ids, owner, mask_table, res_weight, base, modulation, q_weight, k_weight, v_weight
):
    row_count = base.shape[0]
    selector = (
        mask_ids[:, None] == jnp.arange(mask_table.shape[0], dtype=jnp.int32)[None, :]
    ).astype(jnp.bfloat16)
    condition = (
        control.astype(jnp.float32)
        + jnp.dot(selector, mask_table, preferred_element_type=jnp.float32)
    ).astype(jnp.bfloat16)
    residual = jnp.dot(
        lax.all_gather(condition, "seq", axis=0, tiled=True),
        res_weight,
        preferred_element_type=jnp.float32,
    ).astype(jnp.bfloat16)
    total_rows = owner.shape[0]
    inverse = (
        jnp.zeros((total_rows,), jnp.int32).at[owner].set(jnp.arange(total_rows, dtype=jnp.int32))
    )
    relayed = lax.all_to_all(
        jnp.take(residual, inverse, axis=0), "seq", split_axis=0, concat_axis=1, tiled=True
    )
    hidden = base.astype(jnp.float32) + relayed.astype(jnp.float32)
    normed = layer_norm(hidden, modulation)
    joined = jnp.concatenate([q_weight, k_weight, v_weight], axis=1)
    col_width = q_weight.shape[1]
    columns = jnp.dot(
        lax.all_gather(normed, "seq", axis=0, tiled=True),
        joined,
        preferred_element_type=jnp.float32,
    ).astype(jnp.bfloat16)
    q_cols = columns[:, :col_width]
    k_cols = columns[:, col_width : 2 * col_width]
    v_cols = columns[:, 2 * col_width :]
    initial = (
        jnp.full((row_count, HEADS), -1e30, jnp.float32),
        jnp.zeros((row_count, HEADS), jnp.float32),
        jnp.zeros((row_count, HEADS, HEAD_DIM), jnp.float32),
    )
    queries = lax.all_to_all(q_cols, "seq", split_axis=0, concat_axis=1, tiled=True)
    key_rows, values = (
        lax.all_gather(k_cols, "seq", axis=1, tiled=True),
        lax.all_gather(v_cols, "seq", axis=1, tiled=True),
    )
    query_heads = queries.reshape(row_count, HEADS, HEAD_DIM)
    running_max, running_sum, summed = attend_block(initial, (key_rows, values), query_heads)
    attended = (
        (summed / running_sum[:, :, None]).reshape(row_count, HEADS * HEAD_DIM).astype(jnp.bfloat16)
    )
    return (hidden.astype(jnp.bfloat16), attended)


def solution(mesh):
    in_specs = (
        P(("parts", "seq"), None),
        P(("parts", "seq")),
        P("parts"),
        P(),
        P(None, "seq"),
        P(("parts", "seq"), None),
        P(),
        P(None, "seq"),
        P(None, "seq"),
        P(None, "seq"),
    )
    out_specs = (P(("parts", "seq"), None), P(("parts", "seq"), None))
    return jax.shard_map(
        on_device, mesh=mesh, in_specs=in_specs, out_specs=out_specs, check_vma=False
    )
```

profile of v0, /device:TPU:0, one launch (start us, length us, event | category | flops | bytes accessed | tf_op | source)
XLA Modules:
  0.0 110.4 jit_solution(8229619129411165652)
XLA Ops:
  0.6 0.0 copy-start
  0.6 0.8 compare_select_fusion.1
  1.4 1.0 scatter_custom_fusion
  2.4 0.1 broadcast_in_dim.28
  2.5 1.0 fusion.1
  3.5 25.5 %all_gather.12 = bf16[128,3072]{1,0:T(8,128)(2,1)S(1)} all-gather(bf16[8,3072]{1,0:T(8,128)(2,1)S(1)} %fusion.1), channel_id=1, replica_groups=mesh['parts'=2,'seq'=16] {'seq'}, dimensions={0}, use_global_device_ids=true | all-gather | bytes 835584 | tf_op jit(solution)/shard_map/all_gather | solution.py:53
  29.0 0.0 copy-done
  29.0 0.0 copy-start.2
  29.0 0.5 convolution_convert_fusion
  29.5 0.0 copy-start.1
  29.5 0.1 copy.16
  29.6 0.8 gather_fusion
  30.5 0.0 copy-start.3
  30.5 0.0 copy-start.4
  30.5 0.0 copy-start.5
  30.5 0.7 bitcast_select_fusion
  31.2 3.5 %all-to-all-start = ((bf16[16,8,192]{2,1,0:T(8,128)(2,1)}), bf16[16,8,192]{2,1,0:T(8,128)(2,1)S(1)}, u32[]{:S(2)}, u32[]{:S(2)}) async-start(bf16[16,8,192]{2,1,0:T(8,128)(2,1)} %bitcast_select_fusion), calls=%async_computation | async-start | bytes 131072 | tf_op jit(solution)/shard_map/all_to_all | solution.py:61
  34.7 0.0 copy-done.2
  34.8 6.8 %all-to-all-done = bf16[16,8,192]{2,1,0:T(8,128)(2,1)S(1)} async-done(((bf16[16,8,192]{2,1,0:T(8,128)(2,1)}), bf16[16,8,192]{2,1,0:T(8,128)(2,1)S(1)}, u32[]{:S(2)}, u32[]{:S(2)}) %all-to-all-start) | async-done | bytes 49184 | tf_op jit(solution)/shard_map/all_to_all | solution.py:61
  41.7 0.1 reshape.55
  41.8 0.0 copy-done.1
  41.8 0.1 fusion.21
  41.9 0.2 multiply_reduce_fusion
  42.1 0.6 add_convert_fusion
  42.8 19.9 %all_gather.13 = bf16[128,3072]{1,0:T(8,128)(2,1)S(1)} all-gather(bf16[8,3072]{1,0:T(8,128)(2,1)S(1)} %get-tuple-element.2), channel_id=1, replica_groups=mesh['parts'=2,'seq'=16] {'seq'}, dimensions={0}, use_global_device_ids=true | all-gather | bytes 835584 | tf_op jit(solution)/shard_map/all_gather | solution.py:69
  62.7 0.0 copy-done.3
  62.7 0.0 copy-done.4
  62.7 0.0 copy-done.5
  62.7 0.6 fusion.8
  63.4 0.7 copy.18
  64.1 3.5 %all-to-all-start.1 = ((bf16[16,8,96]{2,1,0:T(8,128)(2,1)}), bf16[16,8,96]{2,1,0:T(8,128)(2,1)S(1)}, u32[]{:S(2)}, u32[]{:S(2)}) async-start(bf16[16,8,96]{2,1,0:T(8,128)(2,1)} %bitcast.6), calls=%async_computation.1 | async-start | bytes 65536 | tf_op jit(solution)/shard_map/all_to_all | solution.py:81
  67.6 22.7 %all_gather.15 = bf16[128,1536]{0,1:T(8,128)(2,1)S(1)} all-gather(bf16[128,96]{0,1:T(8,128)(2,1)S(1)} %get-tuple-element.5), channel_id=1, replica_groups=mesh['parts'=2,'seq'=16] {'seq'}, dimensions={1}, use_global_device_ids=true | all-gather | bytes 417792 | tf_op jit(solution)/shard_map/all_gather | solution.py:83
  90.3 18.5 %all_gather.14 = bf16[128,1536]{0,1:T(8,128)(2,1)S(1)} all-gather(bf16[128,96]{0,1:T(8,128)(2,1)S(1)} %get-tuple-element.6), channel_id=1, replica_groups=mesh['parts'=2,'seq'=16] {'seq'}, dimensions={1}, use_global_device_ids=true | all-gather | bytes 417792 | tf_op jit(solution)/shard_map/all_gather | solution.py:84
  108.8 0.0 all-to-all-done.1
  108.8 0.1 reshape.54
  108.9 0.3 fusion.28
  109.2 0.4 convolution_bitcast_fusion
  109.6 0.8 fusion.14
  (12 shorter events, 0.1 us)
Async XLA Ops:
  0.6 28.4 %copy-start = (bf16[3072,192]{0,1:T(8,128)(2,1)S(1)}, bf16[3072,192]{0,1:T(8,128)(2,1)}, u32[]{:S(2)}) copy-start(bf16[3072,192]{0,1:T(8,128)(2,1)} %param.14) | copy-start | bytes 3538948
  29.0 5.7 %copy-start.2 = (f32[2,3072]{1,0:T(2,128)S(1)}, f32[2,3072]{1,0:T(2,128)}, u32[]{:S(2)}) copy-start(f32[2,3072]{1,0:T(2,128)} %param.16) | copy-start | bytes 73732
  29.5 12.2 %copy-start.1 = (bf16[8,3072]{1,0:T(8,128)(2,1)S(1)}, bf16[8,3072]{1,0:T(8,128)(2,1)}, u32[]{:S(2)}) copy-start(bf16[8,3072]{1,0:T(8,128)(2,1)} %param.15) | copy-start | bytes 147460
  30.5 32.2 %copy-start.3 = (bf16[3072,96]{0,1:T(8,128)(2,1)S(1)}, bf16[3072,96]{0,1:T(8,128)(2,1)}, u32[]{:S(2)}) copy-start(bf16[3072,96]{0,1:T(8,128)(2,1)} %param.19) | copy-start | bytes 1769476
  30.5 32.2 %copy-start.4 = (bf16[3072,96]{0,1:T(8,128)(2,1)S(1)}, bf16[3072,96]{0,1:T(8,128)(2,1)}, u32[]{:S(2)}) copy-start(bf16[3072,96]{0,1:T(8,128)(2,1)} %param.18) | copy-start | bytes 1769476
  30.5 32.2 %copy-start.5 = (bf16[3072,96]{0,1:T(8,128)(2,1)S(1)}, bf16[3072,96]{0,1:T(8,128)(2,1)}, u32[]{:S(2)}) copy-start(bf16[3072,96]{0,1:T(8,128)(2,1)} %param.17) | copy-start | bytes 1769476
  31.2 10.4 %all-to-all-start = ((bf16[16,8,192]{2,1,0:T(8,128)(2,1)}), bf16[16,8,192]{2,1,0:T(8,128)(2,1)S(1)}, u32[]{:S(2)}, u32[]{:S(2)}) async-start(bf16[16,8,192]{2,1,0:T(8,128)(2,1)} %bitcast_select_fusion), calls=%async_computation | async-start | bytes 131072 | tf_op jit(solution)/shard_map/all_to_all | solution.py:61
  64.1 44.7 %all-to-all-start.1 = ((bf16[16,8,96]{2,1,0:T(8,128)(2,1)}), bf16[16,8,96]{2,1,0:T(8,128)(2,1)S(1)}, u32[]{:S(2)}, u32[]{:S(2)}) async-start(bf16[16,8,96]{2,1,0:T(8,128)(2,1)} %bitcast.6), calls=%async_computation.1 | async-start | bytes 65536 | tf_op jit(solution)/shard_map/all_to_all | solution.py:81
where the time goes:
time: 111 us; the launch traced here: 110 us
  blocking collectives  86.6 us (78%)
  starting transfers between devices  6.97 us (6%)
  waiting for transfers between devices  6.82 us (6%)
  other arithmetic  3.32 us (3%)
  local copies, waits for them, and re-layouts  3.04 us (3%)
  matrix products  2.81 us (3%)
    all_gather x1, blocking collectives, on_device(): lax.all_gather(condition, 'seq', axis=0, tiled=True)  25.5 us
    all_gather x1, blocking collectives, on_device(): lax.all_gather(k_cols, 'seq', axis=1, tiled=True)  22.7 us
    all_gather x1, blocking collectives, on_device(): lax.all_gather(normed, 'seq', axis=0, tiled=True)  19.9 us
    all_gather x1, blocking collectives, on_device(): lax.all_gather(v_cols, 'seq', axis=1, tiled=True)  18.5 us
    all_to_all x1, waiting for transfers between devices, on_device(): lax.all_to_all(jnp.take(residual, inverse, axis=0), 'seq', split_axis=0,...  6.82 us
    all_to_all x1, starting transfers between devices, on_device(): lax.all_to_all(jnp.take(residual, inverse, axis=0), 'seq', split_axis=0,...  3.48 us
    all_to_all x1, starting transfers between devices, on_device(): lax.all_to_all(q_cols, 'seq', split_axis=0, concat_axis=1, tiled=True)  3.48 us
  transfers between devices with their start and end apart: 2, of which 1 were waited for; matrix products, arithmetic and copies ran while one was open for 0% of the time, Pallas kernels for 0%

commit v1 on v0

--- a/solution.py
+++ b/solution.py
@@ -1,8 +1,11 @@
+import functools
 import math
 
 import jax
 import jax.numpy as jnp
 from jax import lax
+from jax.experimental import pallas as pl
+from jax.experimental.pallas import tpu as pltpu
 from jax.sharding import PartitionSpec as P
 
 HEADS = 12
@@ -91,6 +94,463 @@
     return (hidden.astype(jnp.bfloat16), attended)
 
 
+def remote(src, dst, send_sem, recv_sem, target):
+    return pltpu.make_async_remote_copy(
+        src_ref=src,
+        dst_ref=dst,
+        send_sem=send_sem,
+        recv_sem=recv_sem,
+        device_id={"seq": target},
+        device_id_type=pl.DeviceIdType.MESH,
+    )
+
+
+def dot_last(a, b):
+    return lax.dot_general(
+        a, b, (((1,), (1,)), ((), ())), preferred_element_type=jnp.float32
+    )
+
+
+def one_hot(condition):
+    return jnp.where(condition, 1.0, 0.0).astype(jnp.bfloat16)
+
+
+def fused_kernel(
+    seq,
+    owner_ref,
+    ids_ref,
+    table_ref,
+    mod_ref,
+    control_ref,
+    base_ref,
+    wres_hbm,
+    wq_hbm,
+    wk_hbm,
+    wv_hbm,
+    hid_ref,
+    att_ref,
+    wres,
+    wqkv,
+    cond_all,
+    base_all,
+    hid_all,
+    qkv_own,
+    qkv_mid,
+    part_send,
+    part_recv,
+    out_send,
+    out_recv,
+    load_sem,
+    wsend_sem,
+    wrecv_sem,
+    csend_sem,
+    crecv_sem,
+    bsend_sem,
+    brecv_sem,
+    hsend_sem,
+    hrecv_sem,
+    msend_sem,
+    orecv_sem,
+    mrecv_sem,
+    psend_sem,
+    precv_sem,
+    asend_sem,
+    arecv_sem,
+):
+    me = lax.axis_index("seq")
+    core = lax.rem(me, 2)
+    chip = lax.div(me, 2)
+    row = lax.rem(chip, 2)
+    line = lax.div(chip, 2)
+    chips = seq // 2
+    lines = chips // 2
+    sibling = chip * 2 + 1 - core
+    rows, width = control_ref.shape
+    tokens = rows * seq
+    half = tokens // 2
+    chip_cols = width // chips
+    heads = att_ref.shape[1] // HEAD_DIM
+
+    weights = (wres_hbm, wq_hbm, wk_hbm, wv_hbm)
+
+    def slot(i, which):
+        return wres.at[which] if i == 0 else wqkv.at[i - 1, which]
+
+    loads = [
+        pltpu.make_async_copy(weights[i], slot(i, core), load_sem.at[i]) for i in range(4)
+    ]
+    for load in loads:
+        load.start()
+
+    barrier = pltpu.get_barrier_semaphore()
+    for step in range(1, seq):
+        pl.semaphore_signal(
+            barrier,
+            inc=1,
+            device_id={"seq": lax.rem(me + step, seq)},
+            device_id_type=pl.DeviceIdType.MESH,
+        )
+
+    row_at = lax.broadcasted_iota(jnp.int32, (rows, width), 0)
+    kinds = jnp.zeros((rows, width), jnp.int32)
+    for r in range(rows):
+        kinds = jnp.where(row_at == r, ids_ref[r], kinds)
+    picked = jnp.zeros((rows, width), jnp.float32)
+    for kind in range(table_ref.shape[0]):
+        entry = table_ref[kind : kind + 1, :].astype(jnp.float32)
+        picked = jnp.where(kinds == kind, entry, picked)
+    cond_all[chip] = (control_ref[...].astype(jnp.float32) + picked).astype(jnp.bfloat16)
+    for j in range(chips):
+        base_all[me, j] = base_ref[:, j * chip_cols : (j + 1) * chip_cols]
+
+    pl.semaphore_wait(barrier, seq - 1)
+
+    def along(step):
+        return lax.rem(line + step, lines) * 2
+
+    def gather_sends(buf, send_sem, recv_sem):
+        copies = []
+        for step in range(1, lines):
+            target = (along(step) + row) * 2 + core
+            copies.append(
+                remote(buf.at[chip], buf.at[chip], send_sem.at[step], recv_sem.at[chip], target)
+            )
+        target = (line * 2 + 1 - row) * 2 + core
+        copies.insert(
+            0, remote(buf.at[chip], buf.at[chip], send_sem.at[0], recv_sem.at[chip], target)
+        )
+        for copy in copies:
+            copy.start()
+        return copies
+
+    across = (line * 2 + 1 - row) * 2 + core
+
+    def arrival(buf, send_sem, recv_sem, source):
+        remote(buf.at[source], buf.at[source], send_sem.at[0], recv_sem.at[source], across).wait_recv()
+
+    def forward(buf, send_sem, recv_sem, step):
+        source = along(lines - step) + row
+        arrival(buf, send_sem, recv_sem, source)
+        copy = remote(
+            buf.at[source], buf.at[source], send_sem.at[lines - 1 + step], recv_sem.at[source], across
+        )
+        copy.start()
+        return source, copy
+
+    cond_copies = gather_sends(cond_all, csend_sem, crecv_sem)
+    weight_copies = [
+        remote(weights[i], slot(i, core), wsend_sem.at[i], wrecv_sem.at[i], sibling)
+        for i in range(4)
+    ]
+    weight_copies[0].start()
+
+    base_copies = []
+    for step in range(1, seq):
+        target = lax.rem(me + step, seq)
+        copy = remote(
+            base_all.at[me, lax.div(target, 2)],
+            base_all.at[me, lax.div(target, 2)],
+            bsend_sem.at[step],
+            brecv_sem.at[me],
+            target,
+        )
+        copy.start()
+        base_copies.append(copy)
+    for copy in weight_copies[1:]:
+        copy.start()
+
+    for step in range(1, lines):
+        cond_copies.append(forward(cond_all, csend_sem, crecv_sem, step)[1])
+
+    owned = one_hot(
+        lax.broadcasted_iota(jnp.int32, (tokens, tokens), 0) == owner_ref[...]
+    )
+
+    def control_row(count, first):
+        at = first + lax.broadcasted_iota(jnp.int32, (count, tokens), 0)
+        part = at // half
+        inner = at % half
+        index = (inner // rows) * (2 * rows) + part * rows + inner % rows
+        return one_hot(index == lax.broadcasted_iota(jnp.int32, (count, tokens), 1))
+
+    mine = control_row(half, core * half)
+    base_of = dot_last(mine, owned).astype(jnp.bfloat16)
+
+    loads[0].wait()
+    weight_copies[0].wait_recv()
+    arrival(cond_all, csend_sem, crecv_sem, across // 2)
+    for step in range(1, lines):
+        arrival(cond_all, csend_sem, crecv_sem, along(lines - step) + 1 - row)
+    for step in range(1, seq):
+        source = lax.rem(me + seq - step, seq)
+        remote(
+            base_all.at[source, chip],
+            base_all.at[source, chip],
+            bsend_sem.at[step],
+            brecv_sem.at[source],
+            sibling,
+        ).wait_recv()
+
+    condition = cond_all[...].reshape(half, width)
+    residual = jnp.concatenate(
+        [jnp.dot(condition, wres[which], preferred_element_type=jnp.float32) for which in range(2)],
+        axis=1,
+    ).astype(jnp.bfloat16)
+    base_cols = jnp.concatenate([base_all[s, chip] for s in range(seq)], axis=0)
+    base_rows = jnp.dot(base_of, base_cols, preferred_element_type=jnp.float32)
+    hid_all[chip] = (base_rows + residual.astype(jnp.float32)).astype(jnp.bfloat16)
+
+    hid_copies = gather_sends(hid_all, hsend_sem, hrecv_sem)
+
+    for i in range(1, 4):
+        loads[i].wait()
+        weight_copies[i].wait_recv()
+
+    for step in range(1, lines):
+        hid_copies.append(forward(hid_all, hsend_sem, hrecv_sem, step)[1])
+    arrival(hid_all, hsend_sem, hrecv_sem, across // 2)
+    for step in range(1, lines):
+        arrival(hid_all, hsend_sem, hrecv_sem, along(lines - step) + 1 - row)
+
+    total = jnp.zeros((half, 1), jnp.float32)
+    for j in range(chips):
+        total += jnp.sum(hid_all[j].astype(jnp.float32), axis=1, keepdims=True)
+    mean = total / width
+    total = jnp.zeros((half, 1), jnp.float32)
+    for j in range(chips):
+        centred = hid_all[j].astype(jnp.float32) - mean
+        total += jnp.sum(centred * centred, axis=1, keepdims=True)
+    scale = lax.rsqrt(total / width + 1e-06)
+
+    columns = [[jnp.zeros((half, wqkv.shape[3]), jnp.float32) for _ in range(2)] for _ in range(3)]
+    for j in range(chips):
+        span = slice(j * chip_cols, (j + 1) * chip_cols)
+        block = hid_all[j].astype(jnp.float32)
+        normed = (
+            (block - mean) * scale * (1.0 + mod_ref[1:2, span]) + mod_ref[0:1, span]
+        ).astype(jnp.bfloat16)
+        for i in range(3):
+            for which in range(2):
+                columns[i][which] += jnp.dot(
+                    normed, wqkv[i, which, span, :], preferred_element_type=jnp.float32
+                )
+
+    pad = 2 * HEAD_DIM - 2 * wqkv.shape[3]
+    blank = jnp.zeros((half, pad), jnp.float32)
+    for i in range(3):
+        first = jnp.concatenate([columns[i][0], columns[i][1], blank], axis=1)
+        second = jnp.concatenate([blank, columns[i][0], columns[i][1]], axis=1)
+        own = jnp.where(row == 0, first[:, :HEAD_DIM], second[:, HEAD_DIM:])
+        middle = jnp.where(row == 0, first[:, HEAD_DIM:], second[:, :HEAD_DIM])
+        span = slice(i * HEAD_DIM, (i + 1) * HEAD_DIM)
+        qkv_own[core, :, span] = own.astype(jnp.bfloat16)
+        qkv_mid[row, core, :, span] = middle.astype(jnp.bfloat16)
+
+    middle_at = line * 4 + 1
+    takes_own = core == row
+    takes_middle = jnp.logical_and(row == 0, core == 1)
+    own_copy = remote(
+        qkv_own.at[core], qkv_own.at[core], msend_sem.at[0], orecv_sem, sibling
+    )
+    mid_copy = remote(
+        qkv_mid.at[row, core],
+        qkv_mid.at[row, core],
+        msend_sem.at[1],
+        mrecv_sem.at[row * 2 + core],
+        middle_at,
+    )
+
+    @pl.when(jnp.logical_not(takes_own))
+    def _():
+        own_copy.start()
+
+    @pl.when(jnp.logical_not(takes_middle))
+    def _():
+        mid_copy.start()
+
+    chosen = []
+    for first in (me * rows, sibling * rows):
+        named = one_hot(
+            first + lax.broadcasted_iota(jnp.int32, (rows, tokens), 0) == owner_ref[...]
+        )
+        chosen.append(named)
+    chosen = dot_last(jnp.concatenate(chosen, axis=0), mine).astype(jnp.bfloat16)
+    for j in range(chips):
+        span = slice(j * chip_cols, (j + 1) * chip_cols)
+        piece = jnp.dot(chosen, hid_all[j], preferred_element_type=jnp.float32)
+        hid_ref[:, span] = piece[:rows].astype(jnp.bfloat16)
+        part_send[:, span] = piece[rows:].astype(jnp.bfloat16)
+    part_copy = remote(part_send, part_recv, psend_sem, precv_sem, sibling)
+    part_copy.start()
+
+    to_base = dot_last(owned, control_row(tokens, 0)).astype(jnp.bfloat16)
+
+    def attend(queries, keys, values):
+        queries = jnp.dot(to_base, queries, preferred_element_type=jnp.float32).astype(jnp.bfloat16)
+        scores = dot_last(queries, keys) / math.sqrt(HEAD_DIM)
+        expo = jnp.exp(scores - jnp.max(scores, axis=1, keepdims=True))
+        denom = jnp.sum(expo, axis=1, keepdims=True)
+        summed = jnp.dot(expo.astype(jnp.bfloat16), values, preferred_element_type=jnp.float32)
+        out_send[...] = summed / denom
+
+    head = line * 3 + row + core
+
+    @pl.when(takes_own)
+    def _():
+        remote(
+            qkv_own.at[1 - core], qkv_own.at[1 - core], msend_sem.at[0], orecv_sem, sibling
+        ).wait_recv()
+        joined = jnp.concatenate([qkv_own[0], qkv_own[1]], axis=0)
+        attend(*[joined[:, i * HEAD_DIM : (i + 1) * HEAD_DIM] for i in range(3)])
+
+    @pl.when(takes_middle)
+    def _():
+        for at in ((0, 0), (1, 0), (1, 1)):
+            remote(
+                qkv_mid.at[at[0], at[1]],
+                qkv_mid.at[at[0], at[1]],
+                msend_sem.at[1],
+                mrecv_sem.at[at[0] * 2 + at[1]],
+                sibling,
+            ).wait_recv()
+        joined = jnp.concatenate(
+            [qkv_mid[0, which] + qkv_mid[1, which] for which in range(2)], axis=0
+        )
+        attend(*[joined[:, i * HEAD_DIM : (i + 1) * HEAD_DIM] for i in range(3)])
+
+    works = jnp.logical_or(takes_own, takes_middle)
+
+    def out_copy(step):
+        target = lax.rem(me + step, seq)
+        return remote(
+            out_send.at[pl.ds(pl.multiple_of(target * rows, rows), rows)],
+            out_recv.at[head],
+            asend_sem.at[step],
+            arecv_sem.at[head],
+            target,
+        )
+
+    @pl.when(works)
+    def _():
+        for step in range(1, seq):
+            out_copy(step).start()
+        out_recv[head] = out_send[pl.ds(pl.multiple_of(me * rows, rows), rows), :]
+
+    part_copy.wait_recv()
+    hid_ref[...] = hid_ref[...] + part_recv[...]
+
+    for copy in cond_copies + base_copies + weight_copies + hid_copies:
+        copy.wait_send()
+
+    @pl.when(jnp.logical_not(takes_own))
+    def _():
+        own_copy.wait_send()
+
+    @pl.when(jnp.logical_not(takes_middle))
+    def _():
+        mid_copy.wait_send()
+
+    part_copy.wait_send()
+
+    for h in range(heads):
+        which = h % 3
+        source = (h // 3) * 4 + (0, 1, 3)[which]
+
+        @pl.when(source != me)
+        def _():
+            remote(
+                out_recv.at[h], out_recv.at[h], asend_sem.at[0], arecv_sem.at[h], sibling
+            ).wait_recv()
+
+        att_ref[:, h * HEAD_DIM : (h + 1) * HEAD_DIM] = out_recv[h].astype(jnp.bfloat16)
+
+    @pl.when(works)
+    def _():
+        for step in range(1, seq):
+            out_copy(step).wait_send()
+
+
+def on_device_fused(
+    seq,
+    control, mask_ids, owner, mask_table, res_weight, base, modulation, q_weight, k_weight, v_weight
+):
+    rows, width = control.shape
+    chips = seq // 2
+    heads_width = q_weight.shape[1] * seq
+    fits = (
+        seq % 4 == 0
+        and rows == 8
+        and width % (chips * HEAD_DIM) == 0
+        and q_weight.shape[1] * 8 == 3 * 2 * HEAD_DIM
+        and (rows * seq) % HEAD_DIM == 0
+        and rows * seq <= 256
+    )
+    if not fits:
+        return on_device(
+            control, mask_ids, owner, mask_table, res_weight, base, modulation, q_weight, k_weight, v_weight
+        )
+    tokens = rows * seq
+    half = tokens // 2
+    chip_cols = width // chips
+    bf16 = jnp.bfloat16
+    vmem = pl.BlockSpec(memory_space=pltpu.VMEM)
+    hbm = pl.BlockSpec(memory_space=pl.ANY)
+    dma = pltpu.SemaphoreType.DMA
+    lines = chips // 2
+    return pl.pallas_call(
+        functools.partial(fused_kernel, seq),
+        out_shape=(
+            jax.ShapeDtypeStruct((rows, width), bf16),
+            jax.ShapeDtypeStruct((rows, heads_width), bf16),
+        ),
+        in_specs=[vmem, pl.BlockSpec(memory_space=pltpu.SMEM)] + [vmem] * 4 + [hbm] * 4,
+        out_specs=(vmem, vmem),
+        scratch_shapes=[
+            pltpu.VMEM((2, width, res_weight.shape[1]), bf16),
+            pltpu.VMEM((3, 2, width, q_weight.shape[1]), bf16),
+            pltpu.VMEM((chips, rows, width), bf16),
+            pltpu.VMEM((seq, chips, rows, chip_cols), bf16),
+            pltpu.VMEM((chips, half, chip_cols), bf16),
+            pltpu.VMEM((2, half, 3 * HEAD_DIM), bf16),
+            pltpu.VMEM((2, 2, half, 3 * HEAD_DIM), bf16),
+            pltpu.VMEM((rows, width), bf16),
+            pltpu.VMEM((rows, width), bf16),
+            pltpu.VMEM((tokens, HEAD_DIM), jnp.float32),
+            pltpu.VMEM((heads_width // HEAD_DIM, rows, HEAD_DIM), jnp.float32),
+            dma((4,)),
+            dma((4,)),
+            dma((4,)),
+            dma((2 * lines,)),
+            dma((chips,)),
+            dma((seq,)),
+            dma((seq,)),
+            dma((2 * lines,)),
+            dma((chips,)),
+            dma((2,)),
+            dma(()),
+            dma((4,)),
+            dma(()),
+            dma(()),
+            dma((seq,)),
+            dma((heads_width // HEAD_DIM,)),
+        ],
+        compiler_params=pltpu.CompilerParams(
+            collective_id=0, has_side_effects=True, vmem_limit_bytes=40 * 1024 * 1024
+        ),
+    )(
+        owner.reshape(1, tokens),
+        mask_ids,
+        mask_table,
+        modulation,
+        control,
+        base,
+        res_weight,
+        q_weight,
+        k_weight,
+        v_weight,
+    )
+
+
 def solution(mesh):
     in_specs = (
         P(("parts", "seq"), None),
@@ -105,6 +565,7 @@
         P(None, "seq"),
     )
     out_specs = (P(("parts", "seq"), None), P(("parts", "seq"), None))
+    body = functools.partial(on_device_fused, mesh.shape["seq"])
     return jax.shard_map(
-        on_device, mesh=mesh, in_specs=in_specs, out_specs=out_specs, check_vma=False
-    )
+        body, mesh=mesh, in_specs=in_specs, out_specs=out_specs, check_vma=False
+    )

time: 111 us -> 42.8 us (0.39)
  blocking collectives: 86.6 us -> 0 us
  Pallas kernels: 0 us -> 34.7 us
  starting transfers between devices: 6.97 us -> 0 us
  waiting for transfers between devices: 6.82 us -> 0 us
  local copies, waits for them, and re-layouts: 3.04 us -> 7.16 us
  other arithmetic: 3.32 us -> 0 us
  matrix products: 2.81 us -> 0 us
    all_gather x4 -> x0, blocking collectives: 86.6 us -> none  [the longest x1 25.5 us: on_device(): lax.all_gather(condition, 'seq', axis=0, tiled=True)]
    pallas_call x0 -> x1, Pallas kernels: none -> 34.7 us  [on_device_fused(): pl.pallas_call(functools.partial(fused_kernel, seq), out_shape=(jax.Shape...]
    unnamed x12 -> x24, local copies, waits for them, and re-layouts: 0.04 us -> 7.16 us
    all_to_all x2 -> x0, starting transfers between devices: 6.97 us -> none  [the longest x1 3.48 us: on_device(): lax.all_to_all(jnp.take(residual, inverse, axis=0), 'seq', split_axis=0,...]
    all_to_all x2 -> x0, waiting for transfers between devices: 6.82 us -> none  [the longest x1 6.82 us: on_device(): lax.all_to_all(jnp.take(residual, inverse, axis=0), 'seq', split_axis=0,...]
    dot_general x5 -> x0, matrix products: 2.81 us -> none  [the longest x1 1.03 us: on_device(): jnp.dot(selector, mask_table, preferred_element_type=jnp.float32)]
    select_n x3 -> x0, other arithmetic: 1.46 us -> none  [the longest x1 0.75 us: on_device(): jnp.zeros((total_rows,), jnp.int32).at[owner]]
  transfers between devices with their start and end apart: 2 -> 0, of which waited for: 1 -> 0; matrix products, arithmetic and copies ran while one was open for 0% -> 0% of each run, Pallas kernels for 0% -> 0%
where the time goes in v1:
time: 42.8 us; the launch traced here: 42.6 us
  Pallas kernels  34.7 us (81%)
  local copies, waits for them, and re-layouts  7.16 us (17%)
  between operations  0.77 us (2%)
    pallas_call x1, Pallas kernels, on_device_fused(): pl.pallas_call(functools.partial(fused_kernel, seq), out_shape=(jax.Shape...  34.7 us
    unnamed x24, local copies, waits for them, and re-layouts  7.16 us

profile of v1, /device:TPU:0, one launch (start us, length us, event | category | flops | bytes accessed | tf_op | source)
XLA Modules:
  0.0 42.6 jit_solution(16480343039995465290)
XLA Ops:
  0.6 0.0 copy-start.8
  0.6 0.0 copy-start.7
  0.7 1.5 %copy.13.wq_hbm = bf16[3072,96]{1,0:T(8,128)(2,1)S(1)} copy(bf16[3072,96]{0,1:T(8,128)(2,1)} %param.17) | data formatting | bytes 1179648 | tf_op args[7]
  2.2 0.0 copy-done.7
  2.2 0.4 copy.14.wk_hbm
  2.6 0.0 copy-done.8
  2.6 1.2 %copy.15.wv_hbm = bf16[3072,96]{1,0:T(8,128)(2,1)} copy(bf16[3072,96]{0,1:T(8,128)(2,1)S(1)} %copy-done.8) | data formatting | bytes 1179648 | tf_op args[9]
  3.7 0.0 copy-start.1
  3.8 0.0 copy-start.2
  3.8 0.0 copy-start.3
  3.8 0.0 copy-start.4
  3.8 0.0 copy-start.5
  3.8 0.0 copy-start.6
  3.8 1.7 %copy.12.wres_hbm = bf16[3072,192]{1,0:T(8,128)(2,1)S(1)} copy(bf16[3072,192]{0,1:T(8,128)(2,1)} %param.14) | data formatting | bytes 2359296 | tf_op args[4]
  5.5 0.0 copy-done.1
  5.5 0.0 copy-done.2
  5.5 0.0 copy-done.3
  5.5 0.0 copy-done.4
  5.5 0.0 copy-done.5
  5.5 0.0 copy-done.6
  5.6 0.0 copy-start
  5.6 1.1 %copy-done = bf16[3072,96]{1,0:T(8,128)(2,1)S(1)} copy-done((bf16[3072,96]{1,0:T(8,128)(2,1)S(1)}, bf16[3072,96]{1,0:T(8,128)(2,1)}, u32[]{:S(2)}) %copy-start) | copy-done | bytes 589848
  6.7 34.7 %shard_map.113 = (bf16[8,3072]{1,0:T(8,128)(2,1)S(1)}, bf16[8,1536]{1,0:T(8,128)(2,1)S(1)}) custom-call(s32[1,128]{1,0:T(1,128)S(1)} %bitcast.1, s32[8]{0:T(128)S(1)} %copy-done.6, bf16[3,3072]{1,0:T(4,128)(2,1)S(1)} %copy-done.3, f32[2,3072]{1,0:T(2,128)S(1)} %copy-done.4, bf16[8,3072]{1,0:T(8,128)(2,1)S(1)} %copy-done.1, bf16[8,3072]{1,0:T(8,128)(2,1)S(1)} %copy-done.2, ...), custom_call_target="tpu_custom_call" | custom-call | tf_op jit(solution)/shard_map/pallas_call | solution.py:500
  41.4 0.6 %copy.18 = bf16[8,3072]{1,0:T(8,128)(2,1)} copy(bf16[8,3072]{1,0:T(8,128)(2,1)S(1)} %get-tuple-element.4) | data formatting | bytes 98304
  42.0 0.6 %copy.19 = bf16[8,1536]{1,0:T(8,128)(2,1)} copy(bf16[8,1536]{1,0:T(8,128)(2,1)S(1)} %get-tuple-element.5) | data formatting | bytes 49152
Async XLA Ops:
  0.6 1.9 %copy-start.8 = (bf16[3072,96]{0,1:T(8,128)(2,1)S(1)}, bf16[3072,96]{0,1:T(8,128)(2,1)}, u32[]{:S(2)}) copy-start(bf16[3072,96]{0,1:T(8,128)(2,1)} %param.19) | copy-start | bytes 1769476
  0.6 1.6 %copy-start.7 = (bf16[3072,96]{0,1:T(8,128)(2,1)S(1)}, bf16[3072,96]{0,1:T(8,128)(2,1)}, u32[]{:S(2)}) copy-start(bf16[3072,96]{0,1:T(8,128)(2,1)} %param.18) | copy-start | bytes 1769476
  3.7 1.8 %copy-start.1 = (bf16[8,3072]{1,0:T(8,128)(2,1)S(1)}, bf16[8,3072]{1,0:T(8,128)(2,1)}, u32[]{:S(2)}) copy-start(bf16[8,3072]{1,0:T(8,128)(2,1)} %control_ref.1) | copy-start | bytes 147460
  3.8 1.8 %copy-start.2 = (bf16[8,3072]{1,0:T(8,128)(2,1)S(1)}, bf16[8,3072]{1,0:T(8,128)(2,1)}, u32[]{:S(2)}) copy-start(bf16[8,3072]{1,0:T(8,128)(2,1)} %base_ref.1) | copy-start | bytes 147460
  3.8 1.8 %copy-start.3 = (bf16[3,3072]{1,0:T(4,128)(2,1)S(1)}, bf16[3,3072]{1,0:T(4,128)(2,1)}, u32[]{:S(2)}) copy-start(bf16[3,3072]{1,0:T(4,128)(2,1)} %table_ref.1) | copy-start | bytes 55300
  3.8 1.8 %copy-start.4 = (f32[2,3072]{1,0:T(2,128)S(1)}, f32[2,3072]{1,0:T(2,128)}, u32[]{:S(2)}) copy-start(f32[2,3072]{1,0:T(2,128)} %mod_ref.1) | copy-start | bytes 73732
  3.8 1.8 %copy-start.5 = (s32[128]{0:T(128)S(1)}, s32[128]{0:T(128)}, u32[]{:S(2)}) copy-start(s32[128]{0:T(128)} %param.12) | copy-start | bytes 1540
  3.8 1.8 %copy-start.6 = (s32[8]{0:T(128)S(1)}, s32[8]{0:T(128)}, u32[]{:S(2)}) copy-start(s32[8]{0:T(128)} %ids_ref.1) | copy-start | bytes 100
  5.6 1.1 %copy-start = (bf16[3072,96]{1,0:T(8,128)(2,1)S(1)}, bf16[3072,96]{1,0:T(8,128)(2,1)}, u32[]{:S(2)}) copy-start(bf16[3072,96]{1,0:T(8,128)(2,1)} %copy.15.wv_hbm) | copy-start | bytes 1769476

commit v2 on v1

--- a/solution.py
+++ b/solution.py
@@ -119,16 +119,20 @@
     seq,
     owner_ref,
     ids_ref,
-    table_ref,
-    mod_ref,
-    control_ref,
-    base_ref,
+    table_hbm,
+    mod_hbm,
+    control_hbm,
+    base_hbm,
     wres_hbm,
     wq_hbm,
     wk_hbm,
     wv_hbm,
     hid_ref,
     att_ref,
+    table_ref,
+    mod_ref,
+    control_ref,
+    base_ref,
     wres,
     wqkv,
     cond_all,
@@ -165,7 +169,7 @@
     chips = seq // 2
     lines = chips // 2
     sibling = chip * 2 + 1 - core
-    rows, width = control_ref.shape
+    rows, width = control_hbm.shape
     tokens = rows * seq
     half = tokens // 2
     chip_cols = width // chips
@@ -179,7 +183,15 @@
     loads = [
         pltpu.make_async_copy(weights[i], slot(i, core), load_sem.at[i]) for i in range(4)
     ]
-    for load in loads:
+    inputs = (
+        (control_hbm, control_ref),
+        (table_hbm, table_ref),
+        (base_hbm, base_ref),
+        (mod_hbm, mod_ref),
+    )
+    for i, (source, kept) in enumerate(inputs):
+        loads.append(pltpu.make_async_copy(source, kept, load_sem.at[4 + i]))
+    for load in loads[4:] + loads[:4]:
         load.start()
 
     barrier = pltpu.get_barrier_semaphore()
@@ -191,6 +203,8 @@
             device_id_type=pl.DeviceIdType.MESH,
         )
 
+    for load in loads[4:]:
+        load.wait()
     row_at = lax.broadcasted_iota(jnp.int32, (rows, width), 0)
     kinds = jnp.zeros((rows, width), jnp.int32)
     for r in range(rows):
@@ -268,9 +282,14 @@
 
     def control_row(count, first):
         at = first + lax.broadcasted_iota(jnp.int32, (count, tokens), 0)
-        part = at // half
-        inner = at % half
-        index = (inner // rows) * (2 * rows) + part * rows + inner % rows
+        part = jnp.where(at >= half, 1, 0)
+        inner = at - part * half
+        shift = rows.bit_length() - 1
+        index = (
+            lax.shift_left(lax.shift_right_logical(inner, shift), shift + 1)
+            + part * rows
+            + lax.bitwise_and(inner, rows - 1)
+        )
         return one_hot(index == lax.broadcasted_iota(jnp.int32, (count, tokens), 1))
 
     mine = control_row(half, core * half)
@@ -292,10 +311,7 @@
         ).wait_recv()
 
     condition = cond_all[...].reshape(half, width)
-    residual = jnp.concatenate(
-        [jnp.dot(condition, wres[which], preferred_element_type=jnp.float32) for which in range(2)],
-        axis=1,
-    ).astype(jnp.bfloat16)
+    residual = dot_last(condition, wres[...].reshape(chip_cols, width)).astype(jnp.bfloat16)
     base_cols = jnp.concatenate([base_all[s, chip] for s in range(seq)], axis=0)
     base_rows = jnp.dot(base_of, base_cols, preferred_element_type=jnp.float32)
     hid_all[chip] = (base_rows + residual.astype(jnp.float32)).astype(jnp.bfloat16)
@@ -322,7 +338,8 @@
         total += jnp.sum(centred * centred, axis=1, keepdims=True)
     scale = lax.rsqrt(total / width + 1e-06)
 
-    columns = [[jnp.zeros((half, wqkv.shape[3]), jnp.float32) for _ in range(2)] for _ in range(3)]
+    local = 2 * wqkv.shape[2]
+    columns = [jnp.zeros((half, local), jnp.float32) for _ in range(3)]
     for j in range(chips):
         span = slice(j * chip_cols, (j + 1) * chip_cols)
         block = hid_all[j].astype(jnp.float32)
@@ -330,16 +347,12 @@
             (block - mean) * scale * (1.0 + mod_ref[1:2, span]) + mod_ref[0:1, span]
         ).astype(jnp.bfloat16)
         for i in range(3):
-            for which in range(2):
-                columns[i][which] += jnp.dot(
-                    normed, wqkv[i, which, span, :], preferred_element_type=jnp.float32
-                )
-
-    pad = 2 * HEAD_DIM - 2 * wqkv.shape[3]
-    blank = jnp.zeros((half, pad), jnp.float32)
+            columns[i] += dot_last(normed, wqkv[i, :, :, span].reshape(local, chip_cols))
+
+    blank = jnp.zeros((half, 2 * HEAD_DIM - local), jnp.float32)
     for i in range(3):
-        first = jnp.concatenate([columns[i][0], columns[i][1], blank], axis=1)
-        second = jnp.concatenate([blank, columns[i][0], columns[i][1]], axis=1)
+        first = jnp.concatenate([columns[i], blank], axis=1)
+        second = jnp.concatenate([blank, columns[i]], axis=1)
         own = jnp.where(row == 0, first[:, :HEAD_DIM], second[:, HEAD_DIM:])
         middle = jnp.where(row == 0, first[:, HEAD_DIM:], second[:, :HEAD_DIM])
         span = slice(i * HEAD_DIM, (i + 1) * HEAD_DIM)
@@ -503,11 +516,15 @@
             jax.ShapeDtypeStruct((rows, width), bf16),
             jax.ShapeDtypeStruct((rows, heads_width), bf16),
         ),
-        in_specs=[vmem, pl.BlockSpec(memory_space=pltpu.SMEM)] + [vmem] * 4 + [hbm] * 4,
+        in_specs=[vmem, pl.BlockSpec(memory_space=pltpu.SMEM)] + [hbm] * 8,
         out_specs=(vmem, vmem),
         scratch_shapes=[
-            pltpu.VMEM((2, width, res_weight.shape[1]), bf16),
-            pltpu.VMEM((3, 2, width, q_weight.shape[1]), bf16),
+            pltpu.VMEM(mask_table.shape, bf16),
+            pltpu.VMEM(modulation.shape, jnp.float32),
+            pltpu.VMEM((rows, width), bf16),
+            pltpu.VMEM((rows, width), bf16),
+            pltpu.VMEM((2, res_weight.shape[1], width), bf16),
+            pltpu.VMEM((3, 2, q_weight.shape[1], width), bf16),
             pltpu.VMEM((chips, rows, width), bf16),
             pltpu.VMEM((seq, chips, rows, chip_cols), bf16),
             pltpu.VMEM((chips, half, chip_cols), bf16),
@@ -517,7 +534,7 @@
             pltpu.VMEM((rows, width), bf16),
             pltpu.VMEM((tokens, HEAD_DIM), jnp.float32),
             pltpu.VMEM((heads_width // HEAD_DIM, rows, HEAD_DIM), jnp.float32),
-            dma((4,)),
+            dma((8,)),
             dma((4,)),
             dma((4,)),
             dma((2 * lines,)),
@@ -535,7 +552,7 @@
             dma((heads_width // HEAD_DIM,)),
         ],
         compiler_params=pltpu.CompilerParams(
-            collective_id=0, has_side_effects=True, vmem_limit_bytes=40 * 1024 * 1024
+            collective_id=0, has_side_effects=True, vmem_limit_bytes=56 * 1024 * 1024
         ),
     )(
         owner.reshape(1, tokens),
@@ -544,10 +561,10 @@
         modulation,
         control,
         base,
-        res_weight,
-        q_weight,
-        k_weight,
-        v_weight,
+        res_weight.T,
+        q_weight.T,
+        k_weight.T,
+        v_weight.T,
     )
 
 

time: 42.8 us -> 40.7 us (0.951)
  local copies, waits for them, and re-layouts: 7.16 us -> 2.77 us
  Pallas kernels: 34.7 us -> 37 us
    unnamed x24 -> x2, local copies, waits for them, and re-layouts: 7.16 us -> 2.77 us
    pallas_call x1, Pallas kernels: 34.7 us -> 37 us  [on_device_fused(): pl.pallas_call(functools.partial(fused_kernel, seq), out_shape=(jax.Shape...]
where the time goes in v2:
time: 40.7 us; the launch traced here: 40.4 us
  Pallas kernels  37 us (91%)
  local copies, waits for them, and re-layouts  2.77 us (7%)
  between operations  0.64 us (2%)
    pallas_call x1, Pallas kernels, on_device_fused(): pl.pallas_call(functools.partial(fused_kernel, seq), out_shape=(jax.Shape...  37 us
    unnamed x2, local copies, waits for them, and re-layouts  2.77 us

profile of v2, /device:TPU:0, one launch (start us, length us, event | category | flops | bytes accessed | tf_op | source)
XLA Modules:
  0.0 40.4 jit_solution(6993670350007257956)
XLA Ops:
  0.6 37.0 %shard_map.113 = (bf16[8,3072]{1,0:T(8,128)(2,1)}, bf16[8,1536]{1,0:T(8,128)(2,1)}) custom-call(s32[1,128]{1,0:T(1,128)} %bitcast.9, s32[8]{0:T(128)} %ids_ref.1, bf16[3,3072]{1,0:T(4,128)(2,1)} %table_hbm.1, f32[2,3072]{1,0:T(2,128)} %mod_hbm.1, bf16[8,3072]{1,0:T(8,128)(2,1)} %control_hbm.1, bf16[8,3072]{1,0:T(8,128)(2,1)} %base_hbm.1, ...), custom_call_target="tpu_custom_call" | custom-call | tf_op jit(solution)/shard_map/pallas_call | solution.py:513
  37.6 1.4 %copy.14 = bf16[8,3072]{1,0:T(8,128)(2,1)} copy(bf16[8,3072]{1,0:T(8,128)(2,1)} %get-tuple-element.4) | data formatting | bytes 98304
  39.1 1.3 %copy.15 = bf16[8,1536]{1,0:T(8,128)(2,1)} copy(bf16[8,1536]{1,0:T(8,128)(2,1)} %get-tuple-element.5) | data formatting | bytes 49152

commit v3 on v2

--- a/solution.py
+++ b/solution.py
@@ -322,32 +322,46 @@
         loads[i].wait()
         weight_copies[i].wait_recv()
 
+    local = 2 * wqkv.shape[2]
+    row_of = lax.broadcasted_iota(jnp.int32, (rows, width), 0)
+    affine = jnp.where(row_of == 0, 1.0 + mod_ref[1:2, :], jnp.where(row_of == 1, mod_ref[0:1, :], 0.0))
+    coarse = affine.astype(jnp.bfloat16).astype(jnp.float32)
+    affine = jnp.concatenate([coarse, affine - coarse], axis=0).astype(jnp.bfloat16)
+    affine = [dot_last(affine, wqkv[i].reshape(local, width)) for i in range(3)]
+    affine = [both[:rows] + both[rows:] for both in affine]
+    sums = [jnp.zeros((half, 1), jnp.float32)]
+    columns = [jnp.zeros((half, local), jnp.float32) for _ in range(3)]
+
+    def consume(j):
+        span = pl.ds(pl.multiple_of(j * chip_cols, HEAD_DIM), chip_cols)
+        block = hid_all[j].astype(jnp.float32)
+        sums[0] += jnp.sum(block, axis=1, keepdims=True)
+        gained = (block * (1.0 + mod_ref[1:2, span])).astype(jnp.bfloat16)
+        for i in range(3):
+            columns[i] += dot_last(gained, wqkv[i, :, :, span].reshape(local, chip_cols))
+
+    consume(chip)
     for step in range(1, lines):
-        hid_copies.append(forward(hid_all, hsend_sem, hrecv_sem, step)[1])
-    arrival(hid_all, hsend_sem, hrecv_sem, across // 2)
+        source, copy = forward(hid_all, hsend_sem, hrecv_sem, step)
+        hid_copies.append(copy)
+        if step == 1:
+            arrival(hid_all, hsend_sem, hrecv_sem, across // 2)
+            consume(across // 2)
+        consume(source)
     for step in range(1, lines):
-        arrival(hid_all, hsend_sem, hrecv_sem, along(lines - step) + 1 - row)
-
-    total = jnp.zeros((half, 1), jnp.float32)
-    for j in range(chips):
-        total += jnp.sum(hid_all[j].astype(jnp.float32), axis=1, keepdims=True)
-    mean = total / width
+        source = along(lines - step) + 1 - row
+        arrival(hid_all, hsend_sem, hrecv_sem, source)
+        consume(source)
+
+    mean = sums[0] / width
     total = jnp.zeros((half, 1), jnp.float32)
     for j in range(chips):
         centred = hid_all[j].astype(jnp.float32) - mean
         total += jnp.sum(centred * centred, axis=1, keepdims=True)
     scale = lax.rsqrt(total / width + 1e-06)
-
-    local = 2 * wqkv.shape[2]
-    columns = [jnp.zeros((half, local), jnp.float32) for _ in range(3)]
-    for j in range(chips):
-        span = slice(j * chip_cols, (j + 1) * chip_cols)
-        block = hid_all[j].astype(jnp.float32)
-        normed = (
-            (block - mean) * scale * (1.0 + mod_ref[1:2, span]) + mod_ref[0:1, span]
-        ).astype(jnp.bfloat16)
-        for i in range(3):
-            columns[i] += dot_last(normed, wqkv[i, :, :, span].reshape(local, chip_cols))
+    columns = [
+        (columns[i] - mean * affine[i][0:1]) * scale + affine[i][1:2] for i in range(3)
+    ]
 
     blank = jnp.zeros((half, 2 * HEAD_DIM - local), jnp.float32)
     for i in range(3):

time: 40.7 us -> 39.2 us (0.963)
  Pallas kernels: 37 us -> 35.5 us
    pallas_call x1, Pallas kernels: 37 us -> 35.5 us  [on_device_fused(): pl.pallas_call(functools.partial(fused_kernel, seq), out_shape=(jax.Shape...]
where the time goes in v3:
time: 39.2 us; the launch traced here: 38.9 us
  Pallas kernels  35.5 us (91%)
  local copies, waits for them, and re-layouts  2.77 us (7%)
  between operations  0.64 us (2%)
    pallas_call x1, Pallas kernels, on_device_fused(): pl.pallas_call(functools.partial(fused_kernel, seq), out_shape=(jax.Shape...  35.5 us
    unnamed x2, local copies, waits for them, and re-layouts  2.77 us

profile of v3, /device:TPU:0, one launch (start us, length us, event | category | flops | bytes accessed | tf_op | source)
XLA Modules:
  0.0 38.9 jit_solution(15832049142857399809)
XLA Ops:
  0.6 35.5 %shard_map.113 = (bf16[8,3072]{1,0:T(8,128)(2,1)}, bf16[8,1536]{1,0:T(8,128)(2,1)}) custom-call(s32[1,128]{1,0:T(1,128)} %bitcast.9, s32[8]{0:T(128)} %ids_ref.1, bf16[3,3072]{1,0:T(4,128)(2,1)} %table_hbm.1, f32[2,3072]{1,0:T(2,128)} %mod_hbm.1, bf16[8,3072]{1,0:T(8,128)(2,1)} %control_hbm.1, bf16[8,3072]{1,0:T(8,128)(2,1)} %base_hbm.1, ...), custom_call_target="tpu_custom_call" | custom-call | tf_op jit(solution)/shard_map/pallas_call | solution.py:527
  36.2 1.4 %copy.14 = bf16[8,3072]{1,0:T(8,128)(2,1)} copy(bf16[8,3072]{1,0:T(8,128)(2,1)} %get-tuple-element.4) | data formatting | bytes 98304
  37.6 1.3 %copy.15 = bf16[8,1536]{1,0:T(8,128)(2,1)} copy(bf16[8,1536]{1,0:T(8,128)(2,1)} %get-tuple-element.5) | data formatting | bytes 49152
